TPU v7x, 32 devices: a whole 2x2x4 slice. The times are simulated.
32 devices in a mesh: subtree: 2 (over x), panel: 4 (over y, core), snap: 4 (over z).
Axes of the slice: x: 2, y: 2, z: 4, core: 2. Of those that a mesh axis runs over, the one named last changes fastest.
Arguments:
- leaf_rhs: bfloat16 [8, 1024, 128], P('subtree', 'panel', 'snap'), may hold values from -6 to 6
- upper_rhs: bfloat16 [7, 1024, 128], P(None, 'panel', 'snap'), may hold values from -6 to 6
- leaf_inv: bfloat16 [8, 1024, 1024], P('subtree', 'panel'), may hold values from -1 to 2, as said below
- upper_inv: bfloat16 [7, 1024, 1024], P(None, 'panel'), may hold values from -1 to 2, as said below
- leaf_panels: bfloat16 [8, 3, 1024, 1024], P('subtree', None, 'panel'), may hold values from -0.09375 to 0.09375
- mid_panels: bfloat16 [4, 2, 1024, 1024], P(None, None, 'panel'), may hold values from -0.09375 to 0.09375
- top_panels: bfloat16 [2, 1024, 1024], P(None, 'panel'), may hold values from -0.09375 to 0.09375
- leaf_widths: int32 [8], P('subtree'), may hold values from 256 to 1024
- upper_widths: int32 [7], replicated, may hold values from 256 to 1024
Outputs:
- leaf_solution: bfloat16 [8, 1024, 128], P('subtree', 'panel', 'snap')
- upper_solution: bfloat16 [7, 1024, 128], P(None, 'panel', 'snap')
Inputs may be any that keep to these rules, and one draw needn't show every extreme that they name: `leaf_inv`: each inverse block is a full matrix near the identity. `upper_inv`: each inverse block is a full matrix near the identity.
All inputs are finite; a program needn't handle non-finite values.
Results may differ from a plain program's by a relative error of at most 0.024.
Values may be sent and summed in bfloat16 or wider, within the bound.
A program may use at most 64 MiB of HBM per device.

v0:
```python
import jax
import jax.numpy as jnp
from jax import lax
from jax.sharding import PartitionSpec as P


def live_mask(widths, full_width):
    return (jnp.arange(full_width, dtype=jnp.int32)[None, :] < widths[:, None]).astype(jnp.float32)


def own_rows(mask_full, own_count):
    return lax.dynamic_slice_in_dim(mask_full, lax.axis_index("panel") * own_count, own_count, 1)


def solve_down(inverse, reduced, mask_full):
    own_count = inverse.shape[1]
    live_cols = mask_full.astype(jnp.bfloat16)
    result = jnp.einsum(
        "nrw,nwc->nrc",
        inverse,
        lax.all_gather(reduced, "panel", axis=1, tiled=True) * live_cols[:, :, None],
        preferred_element_type=jnp.float32,
    )
    return (result * own_rows(mask_full, own_count)[:, :, None]).astype(jnp.bfloat16)


def spread(panels, solved):
    return jnp.einsum(
        "nkrw,nwc->nkrc",
        panels,
        lax.all_gather(solved, "panel", axis=1, tiled=True),
        preferred_element_type=jnp.float32,
    )


def ancestor_tables(global_index, level, count_up):
    offsets = [0, 0, 4, 6]
    slot_ids = jnp.arange(7, dtype=jnp.int32)
    tables = []
    for ancestor_rank in range(count_up):
        target = offsets[level + 1 + ancestor_rank] + jnp.right_shift(
            global_index, 1 + ancestor_rank
        )
        tables.append((slot_ids[None, :] == target[:, None]).astype(jnp.float32))
    return tables


def add_coupled(accum, coupled, tables):
    for ancestor_rank in range(len(tables)):
        accum = accum + jnp.einsum(
            "nrc,nu->urc",
            coupled[:, ancestor_rank],
            tables[ancestor_rank],
            precision=lax.Precision.HIGHEST,
        )
    return accum


def solve_up(inverse, panels, solved, upper_x, tables, mask_full):
    own_count = inverse.shape[1]
    if panels is None:
        reduced = solved
    else:
        picked = jnp.stack(
            [
                jnp.einsum(
                    "nu,urc->nrc",
                    table.astype(jnp.bfloat16),
                    upper_x,
                    preferred_element_type=jnp.float32,
                ).astype(jnp.bfloat16)
                for table in tables
            ],
            axis=1,
        )
        carried = lax.psum_scatter(
            jnp.einsum("nkrw,nkrc->wnc", panels, picked, preferred_element_type=jnp.float32).astype(
                jnp.bfloat16
            ),
            "panel",
            scatter_dimension=0,
            tiled=True,
        ).astype(jnp.float32)
        reduced = (solved.astype(jnp.float32) - jnp.transpose(carried, (1, 0, 2))).astype(
            jnp.bfloat16
        )
    own_live = own_rows(mask_full, own_count)
    masked = reduced * own_live[:, :, None].astype(jnp.bfloat16)
    summed = lax.psum_scatter(
        jnp.einsum("nrw,nrc->wnc", inverse, masked, preferred_element_type=jnp.float32).astype(
            jnp.bfloat16
        ),
        "panel",
        scatter_dimension=0,
        tiled=True,
    ).astype(jnp.float32)
    return (jnp.transpose(summed, (1, 0, 2)) * own_live[:, :, None]).astype(jnp.bfloat16)


def per_device(
    leaf_rhs,
    upper_rhs,
    leaf_inv,
    upper_inv,
    leaf_panels,
    mid_panels,
    top_panels,
    leaf_widths,
    upper_widths,
):
    full_width = leaf_inv.shape[2]
    own_count = leaf_inv.shape[1]
    leaf_count = leaf_inv.shape[0]
    groups = lax.axis_size("subtree")
    group_id = lax.axis_index("subtree")
    leaf_live = live_mask(leaf_widths, full_width)
    upper_live = live_mask(upper_widths, full_width)
    leaf_index = group_id * leaf_count + jnp.arange(leaf_count, dtype=jnp.int32)
    upper_index = jnp.arange(7, dtype=jnp.int32)
    leaf_tables = ancestor_tables(leaf_index, 0, 3)
    mid_tables = ancestor_tables(upper_index[0:4], 1, 2)
    high_tables = ancestor_tables(upper_index[4:6] - 4, 2, 1)
    top_stack = top_panels[:, None]
    leaf_sol = solve_down(leaf_inv, leaf_rhs, leaf_live)
    coupled_sum = jnp.zeros((7, own_count, leaf_rhs.shape[2]), jnp.float32)
    coupled_sum = add_coupled(coupled_sum, spread(leaf_panels, leaf_sol), leaf_tables)
    column_share = leaf_rhs.shape[2] // groups
    coupled_sum = lax.psum_scatter(
        coupled_sum.astype(jnp.bfloat16), "subtree", scatter_dimension=2, tiled=True
    ).astype(jnp.float32)
    upper_part = lax.dynamic_slice_in_dim(upper_rhs, group_id * column_share, column_share, 2)
    mid_sol = solve_down(
        upper_inv[0:4],
        (upper_part[0:4].astype(jnp.float32) - coupled_sum[0:4]).astype(jnp.bfloat16),
        upper_live[0:4],
    )
    coupled_sum = add_coupled(coupled_sum, spread(mid_panels, mid_sol), mid_tables)
    high_sol = solve_down(
        upper_inv[4:6],
        (upper_part[4:6].astype(jnp.float32) - coupled_sum[4:6]).astype(jnp.bfloat16),
        upper_live[4:6],
    )
    coupled_sum = add_coupled(coupled_sum, spread(top_stack, high_sol), high_tables)
    root_sol = solve_down(
        upper_inv[6:7],
        (upper_part[6:7].astype(jnp.float32) - coupled_sum[6:7]).astype(jnp.bfloat16),
        upper_live[6:7],
    )
    column_count = upper_part.shape[2]
    zero_mid = jnp.zeros((4, own_count, column_count), jnp.bfloat16)
    zero_high = jnp.zeros((2, own_count, column_count), jnp.bfloat16)
    root_x = solve_up(upper_inv[6:7], None, root_sol, None, None, upper_live[6:7])
    upper_x = jnp.concatenate([zero_mid, zero_high, root_x], axis=0)
    high_x = solve_up(upper_inv[4:6], top_stack, high_sol, upper_x, high_tables, upper_live[4:6])
    upper_x = jnp.concatenate([zero_mid, high_x, root_x], axis=0)
    mid_x = solve_up(upper_inv[0:4], mid_panels, mid_sol, upper_x, mid_tables, upper_live[0:4])
    upper_x = jnp.concatenate([mid_x, high_x, root_x], axis=0)
    upper_x = lax.all_gather(upper_x, "subtree", axis=2, tiled=True)
    leaf_x = solve_up(leaf_inv, leaf_panels, leaf_sol, upper_x, leaf_tables, leaf_live)
    return (leaf_x, upper_x)


def solution(mesh):
    in_specs = (
        P("subtree", "panel", "snap"),
        P(None, "panel", "snap"),
        P("subtree", "panel", None),
        P(None, "panel", None),
        P("subtree", None, "panel", None),
        P(None, None, "panel", None),
        P(None, "panel", None),
        P("subtree"),
        P(),
    )
    out_specs = (P("subtree", "panel", "snap"), P(None, "panel", "snap"))
    return jax.shard_map(
        per_device, mesh=mesh, in_specs=in_specs, out_specs=out_specs, check_vma=False
    )
```

profile of v0, /device:TPU:0, one launch (start us, length us, event | category | flops | bytes accessed | tf_op | source)
XLA Modules:
  0.0 253.7 jit_solution(11947335732800104918)
XLA Ops:
  7.2 0.0 reduce-scatter.9.cloned.1.call-start
  7.3 0.9 fusion.93
  8.1 7.4 %all_gather.24 = bf16[4,1024,32]{1,2,0:T(8,128)(2,1)S(1)} all-gather(bf16[4,256,32]{1,2,0:T(8,128)(2,1)} %param.9), channel_id=1, replica_groups=mesh['subtree'=2,'panel'=4,'snap'=4] {'panel'}, dimensions={1}, use_global_device_ids=true | all-gather | bytes 327680 | tf_op jit(solution)/shard_map/all_gather | solution.py:21
  15.6 0.7 fusion.22
  16.3 5.9 %all_gather.25 = bf16[4,1024,32]{1,2,0:T(8,128)(2,1)S(1)} all-gather(bf16[4,256,32]{1,2,0:T(8,128)(2,1)S(1)} %fusion.22), channel_id=1, replica_groups=mesh['subtree'=2,'panel'=4,'snap'=4] {'panel'}, dimensions={1}, use_global_device_ids=true | all-gather | bytes 327680 | tf_op jit(solution)/shard_map/all_gather | solution.py:31
  22.1 4.8 %convolution_bitcast_fusion.1 = f32[4,3,256,32]{2,3,1,0:T(8,128)S(1)} fusion(bf16[4,3,256,1024]{3,2,1,0:T(8,128)(2,1)} %param.13, bf16[4,1024,32]{1,2,0:T(8,128)(2,1)S(1)} %all_gather.25), kind=kOutput, calls=%fused_computation.7 | convolution fusion | flops 201326592 | bytes 6946816 | tf_op jit(solution)/shard_map/nkrw,nwc->nkrc/dot_general | solution.py:28
  27.0 0.4 fusion.54
  27.4 0.4 convolution_add_fusion.1
  27.8 1.1 fusion.7
  28.8 0.0 reduce-scatter.9.cloned.1.call-update
  28.9 0.0 reduce-scatter.11.cloned.1.call-start
  28.9 0.1 fusion.87
  29.2 0.1 shift-right-arithmetic_add_fusion
  29.3 11.3 %reduce-scatter.9.cloned.1.call-done = bf16[7,256,16]{1,0,2:T(8,128)(2,1)} async-done(((bf16[7,256,32]{1,0,2:T(8,128)(2,1)}), bf16[7,256,16]{1,0,2:T(8,128)(2,1)}) %reduce-scatter.9.cloned.1.call-update) | async-done | bytes 57360 | tf_op jit(solution)/shard_map/reduce_scatter | solution.py:128
  40.6 0.8 convert_element_type.246
  41.5 5.4 %all_gather.26 = bf16[4,1024,16]{1,0,2:T(4,128)(2,1)S(1)} all-gather(bf16[4,256,16]{1,0,2:T(4,128)(2,1)S(1)} %fusion.64), channel_id=1, replica_groups=mesh['subtree'=2,'panel'=4,'snap'=4] {'panel'}, dimensions={1}, use_global_device_ids=true | all-gather | bytes 163840 | tf_op jit(solution)/shard_map/all_gather | solution.py:21
  46.9 2.3 fusion.32
  49.2 5.6 %all_gather.27 = bf16[4,1024,16]{1,2,0:T(8,128)(2,1)S(1)} all-gather(bf16[4,256,16]{1,2,0:T(8,128)(2,1)S(1)} %fusion.32), channel_id=1, replica_groups=mesh['subtree'=2,'panel'=4,'snap'=4] {'panel'}, dimensions={1}, use_global_device_ids=true | all-gather | bytes 163840 | tf_op jit(solution)/shard_map/all_gather | solution.py:31
  54.8 3.4 %convolution_bitcast_fusion.3 = f32[4,2,256,16]{2,3,1,0:T(8,128)S(1)} fusion(bf16[4,2,256,1024]{3,2,1,0:T(8,128)(2,1)} %param.14, bf16[4,1024,16]{1,2,0:T(8,128)(2,1)S(1)} %all_gather.27), kind=kOutput, calls=%fused_computation.18 | convolution fusion | flops 67108864 | bytes 4456448 | tf_op jit(solution)/shard_map/nkrw,nwc->nkrc/dot_general | solution.py:28
  58.2 0.3 convolution_add_fusion.3
  58.5 0.3 convolution_add_fusion.2
  58.9 5.3 %all_gather.28 = bf16[2,1024,16]{1,0,2:T(2,128)(2,1)S(1)} all-gather(bf16[2,256,16]{1,0,2:T(2,128)(2,1)S(1)} %fusion.73), channel_id=1, replica_groups=mesh['subtree'=2,'panel'=4,'snap'=4] {'panel'}, dimensions={1}, use_global_device_ids=true | all-gather | bytes 81920 | tf_op jit(solution)/shard_map/all_gather | solution.py:21
  64.2 1.6 fusion.36
  65.8 5.2 %all_gather.29 = bf16[2,1024,16]{1,2,0:T(8,128)(2,1)S(1)} all-gather(bf16[2,256,16]{1,2,0:T(8,128)(2,1)S(1)} %fusion.36), channel_id=1, replica_groups=mesh['subtree'=2,'panel'=4,'snap'=4] {'panel'}, dimensions={1}, use_global_device_ids=true | all-gather | bytes 81920 | tf_op jit(solution)/shard_map/all_gather | solution.py:31
  71.0 0.4 fusion.142
  71.4 0.3 fusion.83
  71.8 5.3 %all_gather.30 = bf16[1,1024,16]{1,0,2:T(2,128)(2,1)S(1)} all-gather(bf16[1,256,16]{1,0,2:T(2,128)(2,1)S(1)} %fusion.94), channel_id=1, replica_groups=mesh['subtree'=2,'panel'=4,'snap'=4] {'panel'}, dimensions={1}, use_global_device_ids=true | all-gather | bytes 40960 | tf_op jit(solution)/shard_map/all_gather | solution.py:21
  77.0 0.1 broadcast_multiply_fusion.1
  77.1 2.4 fusion.31
  79.5 0.0 reduce-scatter.11.cloned.1.call-update
  79.5 0.0 reduce-scatter.13.cloned.1.call-start
  79.6 0.1 fusion.141
  79.6 19.4 %reduce-scatter.11.cloned.1.call-done = bf16[256,1,16]{0,2,1:T(8,128)(2,1)} async-done(((bf16[1024,1,16]{0,2,1:T(8,128)(2,1)}), bf16[256,1,16]{0,2,1:T(8,128)(2,1)}) %reduce-scatter.11.cloned.1.call-update) | async-done | bytes 8208 | tf_op jit(solution)/shard_map/reduce_scatter | solution.py:89
  99.0 0.7 fusion.91
  99.7 0.2 fusion.61
  99.9 0.1 copy.42
  100.1 0.9 fusion.21
  101.0 0.0 reduce-scatter.15.cloned.1.call-start
  101.1 20.6 %reduce-scatter.13.cloned.1.call-done = bf16[256,2,16]{0,2,1:T(8,128)(2,1)} async-done(((bf16[1024,2,16]{0,2,1:T(8,128)(2,1)}), bf16[256,2,16]{0,2,1:T(8,128)(2,1)}) %reduce-scatter.13.cloned.1.call-update) | async-done | bytes 16400 | tf_op jit(solution)/shard_map/reduce_scatter | solution.py:76
  121.6 2.1 fusion.17
  123.8 0.0 reduce-scatter.17.cloned.1.call-start
  123.8 20.1 %reduce-scatter.15.cloned.1.call-done = bf16[256,2,16]{0,2,1:T(8,128)(2,1)} async-done(((bf16[1024,2,16]{0,2,1:T(8,128)(2,1)}), bf16[256,2,16]{0,2,1:T(8,128)(2,1)}) %reduce-scatter.15.cloned.1.call-update) | async-done | bytes 16400 | tf_op jit(solution)/shard_map/reduce_scatter | solution.py:89
  143.9 0.7 fusion.81
  144.7 0.2 fusion.29
  144.9 0.2 fusion.30
  145.2 3.5 %fusion.15 = bf16[1024,4,16]{0,2,1:T(8,128)(2,1)} fusion(bf16[4,2,256,1024]{3,2,1,0:T(8,128)(2,1)} %param.14, bf16[4,2,256,16]{2,0,3,1:T(4,128)(2,1)S(1)} %pad_maximum_fusion.4), kind=kOutput, calls=%fused_computation.21 | convolution fusion | flops 67174400 | bytes 4390912 | tf_op jit(solution)/shard_map/nkrw,nkrc->wnc/dot_general | solution.py:77
  148.7 0.0 reduce-scatter.19.cloned.1.call-start
  148.7 19.7 %reduce-scatter.17.cloned.1.call-done = bf16[256,4,16]{0,2,1:T(8,128)(2,1)} async-done(((bf16[1024,4,16]{0,2,1:T(8,128)(2,1)}), bf16[256,4,16]{0,2,1:T(8,128)(2,1)}) %reduce-scatter.17.cloned.1.call-update) | async-done | bytes 32784 | tf_op jit(solution)/shard_map/reduce_scatter | solution.py:76
  168.4 2.6 %fusion.12 = bf16[1024,4,16]{0,2,1:T(8,128)(2,1)} fusion(bf16[7,256,1024]{2,1,0:T(8,128)(2,1)} %param.12, bf16[256,4,16]{0,2,1:T(8,128)(2,1)} %reduce-scatter.17.cloned.1.call-done, bf16[4,256,16]{1,2,0:T(8,128)(2,1)S(1)} %fusion.32, bf16[4,256]{1,0:T(4,128)(2,1)S(1)} %get-tuple-element.4), kind=kOutput, calls=%fused_computation.20 | convolution fusion | flops 33701888 | bytes 2295808 | tf_op jit(solution)/shard_map/nrw,nrc->wnc/dot_general | solution.py:90
  171.1 0.0 reduce-scatter.21.cloned.1.call-start
  171.1 19.7 %reduce-scatter.19.cloned.1.call-done = bf16[256,4,16]{0,2,1:T(8,128)(2,1)} async-done(((bf16[1024,4,16]{0,2,1:T(8,128)(2,1)}), bf16[256,4,16]{0,2,1:T(8,128)(2,1)}) %reduce-scatter.19.cloned.1.call-update) | async-done | bytes 32784 | tf_op jit(solution)/shard_map/reduce_scatter | solution.py:89
  190.8 0.8 fusion.65
  191.6 4.9 %all_gather.31 = bf16[7,256,32]{1,2,0:T(8,128)(2,1)S(1)} all-gather(bf16[7,256,16]{1,2,0:T(8,128)(2,1)S(1)} %pad_maximum_fusion.5), channel_id=1, replica_groups=mesh['subtree'=2,'panel'=4,'snap'=4] {'subtree'}, dimensions={2}, use_global_device_ids=true | all-gather | bytes 172032 | tf_op jit(solution)/shard_map/all_gather | solution.py:158
  196.4 0.2 fusion.18
  196.7 0.2 fusion.19
  196.9 0.2 fusion.20
  197.1 0.2 pad_maximum_fusion
  197.3 4.7 %fusion.5 = bf16[1024,4,32]{0,2,1:T(8,128)(2,1)} fusion(bf16[4,3,256,1024]{3,2,1,0:T(8,128)(2,1)} %param.13, bf16[4,3,256,32]{2,0,3,1:T(4,128)(2,1)S(1)} %pad_maximum_fusion), kind=kOutput, calls=%fused_computation.8 | convolution fusion | flops 201457664 | bytes 6750208 | tf_op jit(solution)/shard_map/nkrw,nkrc->wnc/dot_general | solution.py:77
  202.0 0.0 reduce-scatter.23.cloned.1.call-start
  202.1 20.1 %reduce-scatter.21.cloned.1.call-done = bf16[256,4,32]{0,2,1:T(8,128)(2,1)} async-done(((bf16[1024,4,32]{0,2,1:T(8,128)(2,1)}), bf16[256,4,32]{0,2,1:T(8,128)(2,1)}) %reduce-scatter.21.cloned.1.call-update) | async-done | bytes 65552 | tf_op jit(solution)/shard_map/reduce_scatter | solution.py:76
  222.2 2.0 fusion.6
  224.2 20.5 %reduce-scatter.23.cloned.1.call-done = bf16[256,4,32]{0,2,1:T(8,128)(2,1)} async-done(((bf16[1024,4,32]{0,2,1:T(8,128)(2,1)}), bf16[256,4,32]{0,2,1:T(8,128)(2,1)}) %reduce-scatter.23.cloned.1.call-update) | async-done | bytes 65552 | tf_op jit(solution)/shard_map/reduce_scatter | solution.py:89
  244.8 1.5 fusion.49
  246.2 0.6 copy.93
  (50 shorter events, 0.6 us)
Async XLA Ops:
  7.2 8.4 %copy-start = (bf16[4,256,1024]{2,1,0:T(8,128)(2,1)S(1)}, bf16[4,256,1024]{2,1,0:T(8,128)(2,1)}, u32[]{:S(2)}) copy-start(bf16[4,256,1024]{2,1,0:T(8,128)(2,1)} %param.11) | copy-start | bytes 6291460
  7.2 33.4 %reduce-scatter.9.cloned.1.call-start = ((), (), s32[]{:S(2)}) async-start(), calls=%async_computation.8 | async-start | bytes 196608 | tf_op jit(solution)/shard_map/reduce_scatter | solution.py:128
  22.1 6.8 %copy-start.4 = (s32[7]{0:T(128)S(1)}, s32[7]{0:T(128)}, u32[]{:S(2)}) copy-start(s32[7]{0:T(128)} %param.17) | copy-start | bytes 88
  22.1 6.9 %copy-start.3 = (bf16[7,256,32]{1,2,0:T(8,128)(2,1)S(1)}, bf16[7,256,32]{1,2,0:T(8,128)(2,1)}, u32[]{:S(2)}) copy-start(bf16[7,256,32]{1,2,0:T(8,128)(2,1)} %param.10) | copy-start | bytes 344068
  28.9 70.1 %reduce-scatter.11.cloned.1.call-start = ((), (), s32[]{:S(2)}) async-start(), calls=%async_computation.9 | async-start | bytes 40960 | tf_op jit(solution)/shard_map/reduce_scatter | solution.py:89
  46.9 11.3 %copy-start.2 = (bf16[7,256,16]{1,0,2:T(8,128)(2,1)S(1)}, bf16[7,256,16]{1,0,2:T(8,128)(2,1)}, u32[]{:S(2)}) copy-start(bf16[7,256,16]{1,0,2:T(8,128)(2,1)} %reduce-scatter.9.cloned.1.call-done) | copy-start | bytes 172036
  49.2 21.8 %copy-start.1 = (bf16[2,256,1024]{2,1,0:T(8,128)(2,1)S(1)}, bf16[2,256,1024]{2,1,0:T(8,128)(2,1)}, u32[]{:S(2)}) copy-start(bf16[2,256,1024]{2,1,0:T(8,128)(2,1)} %param.15) | copy-start | bytes 3145732
  79.5 42.1 %reduce-scatter.13.cloned.1.call-start = ((), (), s32[]{:S(2)}) async-start(), calls=%async_computation.10 | async-start | bytes 81920 | tf_op jit(solution)/shard_map/reduce_scatter | solution.py:76
  101.0 42.9 %reduce-scatter.15.cloned.1.call-start = ((), (), s32[]{:S(2)}) async-start(), calls=%async_computation.11 | async-start | bytes 81920 | tf_op jit(solution)/shard_map/reduce_scatter | solution.py:89
  123.8 44.6 %reduce-scatter.17.cloned.1.call-start = ((), (), s32[]{:S(2)}) async-start(), calls=%async_computation.12 | async-start | bytes 163840 | tf_op jit(solution)/shard_map/reduce_scatter | solution.py:76
  148.7 42.1 %reduce-scatter.19.cloned.1.call-start = ((), (), s32[]{:S(2)}) async-start(), calls=%async_computation.13 | async-start | bytes 163840 | tf_op jit(solution)/shard_map/reduce_scatter | solution.py:89
  171.1 51.1 %reduce-scatter.21.cloned.1.call-start = ((), (), s32[]{:S(2)}) async-start(), calls=%async_computation.14 | async-start | bytes 327680 | tf_op jit(solution)/shard_map/reduce_scatter | solution.py:76
  202.0 42.7 %reduce-scatter.23.cloned.1.call-start = ((), (), s32[]{:S(2)}) async-start(), calls=%async_computation.15 | async-start | bytes 327680 | tf_op jit(solution)/shard_map/reduce_scatter | solution.py:89
Sparse Core Ops, SparseCore 0:
  29.0 11.5 reduce-scatter.8
  79.6 19.3 reduce-scatter.10
  102.1 19.4 reduce-scatter.12
  124.5 19.4 reduce-scatter.14
  148.8 19.5 reduce-scatter.16
  171.2 19.5 reduce-scatter.18
  202.1 20.0 reduce-scatter.20
  224.7 20.0 reduce-scatter.22
where the time goes:
time: 255 us; the launch traced here: 254 us
  waiting for transfers between devices  151 us (59%)
  blocking collectives  44.9 us (18%)
  matrix products  35.5 us (14%)
  between operations  14.5 us (6%)
  other arithmetic  6.07 us (2%)
    reduce_scatter x4, waiting for transfers between devices, solve_up(): lax.psum_scatter(jnp.einsum('nrw,nrc->wnc', inverse, masked, preferred_el...  79.6 us
    reduce_scatter x3, waiting for transfers between devices, solve_up(): lax.psum_scatter(jnp.einsum('nkrw,nkrc->wnc', panels, picked, preferred_e...  60.4 us
    all_gather x4, blocking collectives, solve_down(): lax.all_gather(reduced, 'panel', axis=1, tiled=True) * live_cols[:, :, None]  23.4 us
    all_gather x3, blocking collectives, spread(): lax.all_gather(solved, 'panel', axis=1, tiled=True)  16.7 us
    reduce_scatter x1, waiting for transfers between devices, per_device(): lax.psum_scatter(coupled_sum.astype(jnp.bfloat16), 'subtree', scatter_dim...  11.3 us
    dot_general x4, matrix products, solve_up(): jnp.einsum('nrw,nrc->wnc', inverse, masked, preferred_element_type=jnp.fl...  9.13 us
    dot_general x3, matrix products, solve_up(): jnp.einsum('nkrw,nkrc->wnc', panels, picked, preferred_element_type=jnp.f...  9.09 us
    dot_general x3, matrix products, spread(): jnp.einsum('nkrw,nwc->nkrc', panels, lax.all_gather(solved, 'panel', axis...  8.51 us
  transfers between devices with their start and end apart: 8, of which 8 were waited for; matrix products, arithmetic and copies ran while one was open for 0% of the time, Pallas kernels for 0%

commit v1 on v0

--- a/solution.py
+++ b/solution.py
@@ -2,6 +2,28 @@
 import jax.numpy as jnp
 from jax import lax
 from jax.sharding import PartitionSpec as P
+
+
+def in_order(blocks, dim):
+    dims = list(blocks.shape[1:])
+    dims[dim] *= blocks.shape[0]
+    return jnp.moveaxis(blocks, 0, dim).reshape(dims)
+
+
+def gather_around(x, axis, dim):
+    size = lax.axis_size(axis)
+    pairs = [(i, (i + 1) % size) for i in range(size)]
+    back = [(b, a) for a, b in pairs]
+    lower, upper = ([], [])
+    for turn in range(size - 1):
+        if turn % 2 == 0:
+            lower.append(lax.ppermute(lower[-1] if lower else x, axis, pairs))
+        else:
+            upper.append(lax.ppermute(upper[-1] if upper else x, axis, back))
+    blocks = jnp.stack([*lower[::-1], x, *upper])
+    shift = lax.axis_index(axis) - len(lower)
+    blocks = blocks[(jnp.arange(size) - shift) % size]
+    return in_order(blocks, dim)
 
 
 def live_mask(widths, full_width):
@@ -18,7 +40,7 @@
     result = jnp.einsum(
         "nrw,nwc->nrc",
         inverse,
-        lax.all_gather(reduced, "panel", axis=1, tiled=True) * live_cols[:, :, None],
+        gather_around(reduced, "panel", 1) * live_cols[:, :, None],
         preferred_element_type=jnp.float32,
     )
     return (result * own_rows(mask_full, own_count)[:, :, None]).astype(jnp.bfloat16)

time: 255 us -> 277 us (1.086)
  blocking collectives: 44.9 us -> 22.6 us
  local copies, waits for them, and re-layouts: 1.02 us -> 20.5 us
  waiting for transfers between devices: 151 us -> 164 us
  starting transfers between devices: 0.33 us -> 9.14 us
  other arithmetic: 6.07 us -> 9.13 us
    all_gather x4 -> x0, blocking collectives: 23.4 us -> none  [solve_down(): lax.all_gather(reduced, 'panel', axis=1, tiled=True) * live_cols[:, :, None]]
    reduce_scatter x4 -> x3, waiting for transfers between devices: 79.6 us -> 59.5 us  [solve_up(): lax.psum_scatter(jnp.einsum('nrw,nrc->wnc', inverse, masked, preferred_el...]
    unnamed x8 -> x9, waiting for transfers between devices: 0.13 us -> 20.3 us
    unnamed x13 -> x50, local copies, waits for them, and re-layouts: 0.69 us -> 15.2 us
    ppermute x0 -> x12, waiting for transfers between devices: none -> 14.4 us  [the longest x8 14.2 us: gather_around(): lower.append(lax.ppermute(lower[-1] if lower else x, axis, pairs))]
    ppermute x0 -> x12, starting transfers between devices: none -> 8.63 us  [the longest x4 6.61 us: gather_around(): upper.append(lax.ppermute(upper[-1] if upper else x, axis, back))]
  transfers between devices with their start and end apart: 8 -> 20, of which waited for: 8 -> 17; matrix products, arithmetic and copies ran while one was open for 0% -> 2% of each run, Pallas kernels for 0% -> 0%
where the time goes in v1:
time: 277 us; the launch traced here: 276 us
  waiting for transfers between devices  164 us (59%)
  matrix products  36 us (13%)
  blocking collectives  22.6 us (8%)
  local copies, waits for them, and re-layouts  20.5 us (7%)
  between operations  14.7 us (5%)
  starting transfers between devices  9.14 us (3%)
  other arithmetic  9.13 us (3%)
    reduce_scatter x3, waiting for transfers between devices, solve_up(): lax.psum_scatter(jnp.einsum('nkrw,nkrc->wnc', panels, picked, preferred_e...  59.8 us
    reduce_scatter x3, waiting for transfers between devices, solve_up(): lax.psum_scatter(jnp.einsum('nrw,nrc->wnc', inverse, masked, preferred_el...  59.5 us
    unnamed x9, waiting for transfers between devices  20.3 us
    all_gather x3, blocking collectives, spread(): lax.all_gather(solved, 'panel', axis=1, tiled=True)  17.8 us
    unnamed x50, local copies, waits for them, and re-layouts  15.2 us
    ppermute x8, waiting for transfers between devices, gather_around(): lower.append(lax.ppermute(lower[-1] if lower else x, axis, pairs))  14.2 us
    reduce_scatter x1, waiting for transfers between devices, per_device(): lax.psum_scatter(coupled_sum.astype(jnp.bfloat16), 'subtree', scatter_dim...  9.73 us
    dot_general x3, matrix products, solve_up(): jnp.einsum('nkrw,nkrc->wnc', panels, picked, preferred_element_type=jnp.f...  9.05 us
  transfers between devices with their start and end apart: 20, of which 17 were waited for; matrix products, arithmetic and copies ran while one was open for 2% of the time, Pallas kernels for 0%

profile of v1, /device:TPU:0, one launch (start us, length us, event | category | flops | bytes accessed | tf_op | source)
XLA Modules:
  0.0 275.8 jit_solution(2212084545742403092)
XLA Ops:
  7.2 0.5 collective-permute-start
  7.7 2.0 collective-permute-start.2
  9.8 0.7 fusion.89
  10.5 0.7 fusion.82
  11.3 0.6 fusion.136
  11.9 0.7 collective-permute-start.1
  12.6 3.1 %collective-permute-done.1 = bf16[4,256,32]{1,2,0:T(8,128)(2,1)S(1)} collective-permute-done((bf16[4,256,32]{1,2,0:T(8,128)(2,1)S(1)}, bf16[4,256,32]{1,2,0:T(8,128)(2,1)S(1)}, u32[]{:S(2)}, u32[]{:S(2)}) %collective-permute-start.1) | collective-permute-done | bytes 65568 | tf_op jit(solution)/shard_map/ppermute | solution.py:20
  15.6 0.9 pad_maximum_fusion
  16.5 0.6 gather_fusion
  17.1 0.7 fusion.22
  17.8 7.1 %all_gather.12 = bf16[4,1024,32]{1,2,0:T(8,128)(2,1)S(1)} all-gather(bf16[4,256,32]{1,2,0:T(8,128)(2,1)S(1)} %fusion.22), channel_id=1, replica_groups=mesh['subtree'=2,'panel'=4,'snap'=4] {'panel'}, dimensions={1}, use_global_device_ids=true | all-gather | bytes 327680 | tf_op jit(solution)/shard_map/all_gather | solution.py:53
  24.9 4.7 %convolution_bitcast_fusion.1 = f32[4,3,256,32]{2,3,1,0:T(8,128)S(1)} fusion(bf16[4,3,256,1024]{3,2,1,0:T(8,128)(2,1)} %param.13, bf16[4,1024,32]{1,2,0:T(8,128)(2,1)S(1)} %all_gather.12), kind=kOutput, calls=%fused_computation.11 | convolution fusion | flops 201326592 | bytes 6946816 | tf_op jit(solution)/shard_map/nkrw,nwc->nkrc/dot_general | solution.py:50
  30.1 0.4 convolution_add_fusion.1
  30.6 1.1 fusion.7
  31.7 0.8 constant_dynamic-slice_fusion.1
  32.5 0.5 shift-right-arithmetic_add_fusion.1
  33.0 9.7 %reduce-scatter.11.cloned.1.call-done = bf16[7,256,16]{1,0,2:T(8,128)(2,1)} async-done(((bf16[7,256,32]{1,0,2:T(8,128)(2,1)}), bf16[7,256,16]{1,0,2:T(8,128)(2,1)}) %reduce-scatter.11.cloned.1.call-update) | async-done | bytes 57360 | tf_op jit(solution)/shard_map/reduce_scatter | solution.py:150
  42.8 0.8 convert_element_type.246
  43.7 0.6 shift-right-arithmetic_add_fusion
  44.3 1.7 collective-permute-start.5
  46.0 1.0 collective-permute-done.3
  47.0 0.7 constant_dynamic-slice_fusion
  47.8 2.6 collective-permute-done.4
  50.5 0.7 gather_fusion.1
  51.4 2.2 fusion.32
  53.6 5.4 %all_gather.13 = bf16[4,1024,16]{1,2,0:T(8,128)(2,1)S(1)} all-gather(bf16[4,256,16]{1,2,0:T(8,128)(2,1)S(1)} %fusion.32), channel_id=1, replica_groups=mesh['subtree'=2,'panel'=4,'snap'=4] {'panel'}, dimensions={1}, use_global_device_ids=true | all-gather | bytes 163840 | tf_op jit(solution)/shard_map/all_gather | solution.py:53
  59.1 3.5 %convolution_bitcast_fusion.3 = f32[4,2,256,16]{2,3,1,0:T(8,128)S(1)} fusion(bf16[4,2,256,1024]{3,2,1,0:T(8,128)(2,1)} %param.14, bf16[4,1024,16]{1,2,0:T(8,128)(2,1)S(1)} %all_gather.13), kind=kOutput, calls=%fused_computation.22 | convolution fusion | flops 67108864 | bytes 4456448 | tf_op jit(solution)/shard_map/nkrw,nwc->nkrc/dot_general | solution.py:50
  63.7 0.7 constant_dynamic-slice_fusion.5
  64.4 1.4 collective-permute-start.8
  65.8 0.7 collective-permute-done.6
  66.5 0.6 fusion.138
  67.2 2.4 collective-permute-done.7
  69.8 0.8 gather_fusion.2
  70.7 1.6 fusion.36
  72.3 5.2 %all_gather.14 = bf16[2,1024,16]{1,2,0:T(8,128)(2,1)S(1)} all-gather(bf16[2,256,16]{1,2,0:T(8,128)(2,1)S(1)} %fusion.36), channel_id=1, replica_groups=mesh['subtree'=2,'panel'=4,'snap'=4] {'panel'}, dimensions={1}, use_global_device_ids=true | all-gather | bytes 81920 | tf_op jit(solution)/shard_map/all_gather | solution.py:53
  77.9 0.9 fusion.78
  79.3 1.5 collective-permute-start.11
  80.8 1.3 collective-permute-done.9
  82.2 3.0 %collective-permute-done.10 = bf16[1,256,16]{1,0,2:T(2,128)(2,1)S(1)} collective-permute-done((bf16[1,256,16]{1,0,2:T(2,128)(2,1)S(1)}, bf16[1,256,16]{1,0,2:T(2,128)(2,1)S(1)}, u32[]{:S(2)}, u32[]{:S(2)}) %collective-permute-start.10) | collective-permute-done | bytes 8224 | tf_op jit(solution)/shard_map/ppermute | solution.py:20
  85.3 0.7 gather_fusion.3
  86.0 2.4 fusion.31
  88.6 19.3 %reduce-scatter.13.cloned.1.call-done = bf16[256,1,16]{0,2,1:T(8,128)(2,1)} async-done(((bf16[1024,1,16]{0,2,1:T(8,128)(2,1)}), bf16[256,1,16]{0,2,1:T(8,128)(2,1)}) %reduce-scatter.13.cloned.1.call-update) | async-done | bytes 8208 | tf_op jit(solution)/shard_map/reduce_scatter | solution.py:111
  107.9 0.7 fusion.86
  108.6 0.8 convolution_convert_fusion.9
  109.4 0.9 fusion.17
  110.6 19.9 %reduce-scatter.15.cloned.1.call-done = bf16[256,2,16]{0,2,1:T(8,128)(2,1)} async-done(((bf16[1024,2,16]{0,2,1:T(8,128)(2,1)}), bf16[256,2,16]{0,2,1:T(8,128)(2,1)}) %reduce-scatter.15.cloned.1.call-update) | async-done | bytes 16400 | tf_op jit(solution)/shard_map/reduce_scatter | solution.py:98
  130.5 1.5 fusion.18
  132.0 4.8 %copy.108 = bf16[1024,2,16]{1,2,0:T(8,128)(2,1)} copy(bf16[1024,2,16]{0,2,1:T(8,128)(2,1)S(1)} %fusion.18) | data formatting | bytes 131072
  136.8 6.5 %reshape.302 = bf16[1024,32]{1,0:T(8,128)(2,1)} reshape(bf16[1024,16,2]{2,1,0:T(8,128)(2,1)} %bitcast.206) | data formatting | bytes 131072
  143.4 20.1 %reduce-scatter.25.cloned.1.call-done = bf16[256,32]{1,0:T(8,128)(2,1)} async-done(((bf16[1024,32]{1,0:T(8,128)(2,1)}), bf16[256,32]{1,0:T(8,128)(2,1)}) %reduce-scatter.25.cloned.1.call-update) | async-done | bytes 16400
  163.5 2.2 reshape.303
  165.7 0.9 copy.109
  167.2 3.5 %fusion.15 = bf16[1024,4,16]{0,2,1:T(8,128)(2,1)} fusion(bf16[4,2,256,1024]{3,2,1,0:T(8,128)(2,1)} %param.14, bf16[4,2,256,16]{2,0,3,1:T(4,128)(2,1)S(1)} %pad_maximum_fusion.7), kind=kOutput, calls=%fused_computation.25 | convolution fusion | flops 67174400 | bytes 4390912 | tf_op jit(solution)/shard_map/nkrw,nkrc->wnc/dot_general | solution.py:99
  170.8 19.7 %reduce-scatter.17.cloned.1.call-done = bf16[256,4,16]{0,2,1:T(8,128)(2,1)} async-done(((bf16[1024,4,16]{0,2,1:T(8,128)(2,1)}), bf16[256,4,16]{0,2,1:T(8,128)(2,1)}) %reduce-scatter.17.cloned.1.call-update) | async-done | bytes 32784 | tf_op jit(solution)/shard_map/reduce_scatter | solution.py:98
  190.5 2.6 fusion.12
  193.2 19.7 %reduce-scatter.19.cloned.1.call-done = bf16[256,4,16]{0,2,1:T(8,128)(2,1)} async-done(((bf16[1024,4,16]{0,2,1:T(8,128)(2,1)}), bf16[256,4,16]{0,2,1:T(8,128)(2,1)}) %reduce-scatter.19.cloned.1.call-update) | async-done | bytes 32784 | tf_op jit(solution)/shard_map/reduce_scatter | solution.py:111
  212.9 0.8 fusion.63
  213.7 4.9 %all_gather.15 = bf16[7,256,32]{1,2,0:T(8,128)(2,1)S(1)} all-gather(bf16[7,256,16]{1,2,0:T(8,128)(2,1)S(1)} %pad_maximum_fusion.8), channel_id=1, replica_groups=mesh['subtree'=2,'panel'=4,'snap'=4] {'subtree'}, dimensions={2}, use_global_device_ids=true | all-gather | bytes 172032 | tf_op jit(solution)/shard_map/all_gather | solution.py:180
  219.4 4.7 %fusion.5 = bf16[1024,4,32]{0,2,1:T(8,128)(2,1)} fusion(bf16[4,3,256,1024]{3,2,1,0:T(8,128)(2,1)} %param.13, bf16[4,3,256,32]{2,0,3,1:T(4,128)(2,1)S(1)} %pad_maximum_fusion.1), kind=kOutput, calls=%fused_computation.12 | convolution fusion | flops 201457664 | bytes 6750208 | tf_op jit(solution)/shard_map/nkrw,nkrc->wnc/dot_general | solution.py:99
  224.2 20.2 %reduce-scatter.21.cloned.1.call-done = bf16[256,4,32]{0,2,1:T(8,128)(2,1)} async-done(((bf16[1024,4,32]{0,2,1:T(8,128)(2,1)}), bf16[256,4,32]{0,2,1:T(8,128)(2,1)}) %reduce-scatter.21.cloned.1.call-update) | async-done | bytes 65552 | tf_op jit(solution)/shard_map/reduce_scatter | solution.py:98
  244.3 2.0 fusion.6
  246.4 20.5 %reduce-scatter.23.cloned.1.call-done = bf16[256,4,32]{0,2,1:T(8,128)(2,1)} async-done(((bf16[1024,4,32]{0,2,1:T(8,128)(2,1)}), bf16[256,4,32]{0,2,1:T(8,128)(2,1)}) %reduce-scatter.23.cloned.1.call-update) | async-done | bytes 65552 | tf_op jit(solution)/shard_map/reduce_scatter | solution.py:111
  266.9 1.5 fusion.49
  268.3 0.6 copy.161
  (120 shorter events, 5.5 us)
Async XLA Ops:
  7.2 9.9 %copy-start = (bf16[4,256,1024]{2,1,0:T(8,128)(2,1)S(1)}, bf16[4,256,1024]{2,1,0:T(8,128)(2,1)}, u32[]{:S(2)}) copy-start(bf16[4,256,1024]{2,1,0:T(8,128)(2,1)} %param.11) | copy-start | bytes 6291460
  7.2 35.6 %reduce-scatter.11.cloned.1.call-start = ((), (), s32[]{:S(2)}) async-start(), calls=%async_computation.8 | async-start | bytes 196608 | tf_op jit(solution)/shard_map/reduce_scatter | solution.py:150
  7.2 4.6 %collective-permute-start = (bf16[4,256,32]{1,2,0:T(8,128)(2,1)}, bf16[4,256,32]{1,2,0:T(8,128)(2,1)S(1)}, u32[]{:S(2)}, u32[]{:S(2)}) collective-permute-start(bf16[4,256,32]{1,2,0:T(8,128)(2,1)} %param.9), channel_id=1, source_target_pairs={{0,4},{4,8},{8,12},{12,0},{1,5},{5,9},{9,13},{13,1},{2,6},{6,10},{... | collective-permute-start | bytes 196616 | tf_op jit(solution)/shard_map/ppermute | solution.py:20
  7.7 4.8 %collective-permute-start.2 = (bf16[4,256,32]{1,2,0:T(8,128)(2,1)}, bf16[4,256,32]{1,2,0:T(8,128)(2,1)S(1)}, u32[]{:S(2)}, u32[]{:S(2)}) collective-permute-start(bf16[4,256,32]{1,2,0:T(8,128)(2,1)} %param.9), channel_id=1, source_target_pairs={{4,0},{8,4},{12,8},{0,12},{5,1},{9,5},{13,9},{1,13},{6,2},{10,6},{... | collective-permute-start | bytes 196616 | tf_op jit(solution)/shard_map/ppermute | solution.py:22
  9.8 40.7 %copy-start.7 = (s32[1024]{0:T(1024)}, s32[1024]{0:T(1024)S(1)}, u32[]{:S(2)}) copy-start(s32[1024]{0:T(1024)S(1)} %pad_clamp_fusion) | copy-start | bytes 12292
  11.8 17.8 %copy-start.3 = (f32[4,256]{1,0:T(4,128)}, f32[4,256]{1,0:T(4,128)S(1)}, u32[]{:S(2)}) copy-start(f32[4,256]{1,0:T(4,128)S(1)} %get-tuple-element.3) | copy-start | bytes 12292
  11.8 39.5 %copy-start.5 = (f32[4,256]{1,0:T(4,128)}, f32[4,256]{1,0:T(4,128)S(1)}, u32[]{:S(2)}) copy-start(f32[4,256]{1,0:T(4,128)S(1)} %get-tuple-element.20) | copy-start | bytes 12292
  11.8 17.9 %copy-start.10 = (s32[4]{0:T(128)}, s32[4]{0:T(128)S(1)}, u32[]{:S(2)}) copy-start(s32[4]{0:T(128)S(1)} %get-tuple-element.22) | copy-start | bytes 52
  11.9 18.3 %copy-start.14 = (s32[4]{0:T(128)}, s32[4]{0:T(128)S(1)}, u32[]{:S(2)}) copy-start(s32[4]{0:T(128)S(1)} %get-tuple-element.21) | copy-start | bytes 52
  11.9 3.7 %collective-permute-start.1 = (bf16[4,256,32]{1,2,0:T(8,128)(2,1)S(1)}, bf16[4,256,32]{1,2,0:T(8,128)(2,1)S(1)}, u32[]{:S(2)}, u32[]{:S(2)}) collective-permute-start(bf16[4,256,32]{1,2,0:T(8,128)(2,1)S(1)} %collective-permute-done), channel_id=1, source_target_pairs={{0,4},{4,8},{8,12},{12,0},{1,5},{5,9},{9,13},{13,1},{2,6},{6,10},{... | collective-permute-start | bytes 196616 | tf_op jit(solution)/shard_map/ppermute | solution.py:20
  12.5 18.0 %copy-start.12 = (s32[4]{0:T(128)}, s32[4]{0:T(128)S(1)}, u32[]{:S(2)}) copy-start(s32[4]{0:T(128)S(1)} %shift-right-arithmetic_add_fusion.3) | copy-start | bytes 52
  31.7 76.2 %reduce-scatter.13.cloned.1.call-start = ((), (), s32[]{:S(2)}) async-start(), calls=%async_computation.9 | async-start | bytes 40960 | tf_op jit(solution)/shard_map/reduce_scatter | solution.py:111
  33.0 29.5 %copy-start.16 = (s32[4]{0:T(128)}, s32[4]{0:T(128)S(1)}, u32[]{:S(2)}) copy-start(s32[4]{0:T(128)S(1)} %get-tuple-element.16) | copy-start | bytes 52
  43.6 3.4 %collective-permute-start.3 = (bf16[4,256,16]{1,0,2:T(4,128)(2,1)S(1)}, bf16[4,256,16]{1,0,2:T(4,128)(2,1)S(1)}, u32[]{:S(2)}, u32[]{:S(2)}) collective-permute-start(bf16[4,256,16]{1,0,2:T(4,128)(2,1)S(1)} %fusion.62), channel_id=1, source_target_pairs={{0,4},{4,8},{8,12},{12,0},{1,5},{5,9},{9,13},{13,1},{2,6},{6,10},{... | collective-permute-start | bytes 98312 | tf_op jit(solution)/shard_map/ppermute | solution.py:20
  44.3 3.5 %collective-permute-start.5 = (bf16[4,256,16]{1,0,2:T(4,128)(2,1)S(1)}, bf16[4,256,16]{1,0,2:T(4,128)(2,1)S(1)}, u32[]{:S(2)}, u32[]{:S(2)}) collective-permute-start(bf16[4,256,16]{1,0,2:T(4,128)(2,1)S(1)} %fusion.62), channel_id=1, source_target_pairs={{4,0},{8,4},{12,8},{0,12},{5,1},{9,5},{13,9},{1,13},{6,2},{10,6},{... | collective-permute-start | bytes 98312 | tf_op jit(solution)/shard_map/ppermute | solution.py:22
  47.0 3.3 %collective-permute-start.4 = (bf16[4,256,16]{1,0,2:T(4,128)(2,1)S(1)}, bf16[4,256,16]{1,0,2:T(4,128)(2,1)S(1)}, u32[]{:S(2)}, u32[]{:S(2)}) collective-permute-start(bf16[4,256,16]{1,0,2:T(4,128)(2,1)S(1)} %collective-permute-done.3), channel_id=1, source_target_pairs={{0,4},{4,8},{8,12},{12,0},{1,5},{5,9},{9,13},{13,1},{2,6},{6,10},{... | collective-permute-start | bytes 98312 | tf_op jit(solution)/shard_map/ppermute | solution.py:20
  51.4 11.2 %copy-start.2 = (bf16[7,256,16]{1,0,2:T(8,128)(2,1)S(1)}, bf16[7,256,16]{1,0,2:T(8,128)(2,1)}, u32[]{:S(2)}) copy-start(bf16[7,256,16]{1,0,2:T(8,128)(2,1)} %reduce-scatter.11.cloned.1.call-done) | copy-start | bytes 172036
  51.4 11.5 %copy-start.18 = (s32[4]{0:T(128)S(1)}, s32[4]{0:T(128)}, u32[]{:S(2)}) copy-start(s32[4]{0:T(128)} %get-tuple-element.15) | copy-start | bytes 52
  59.1 18.5 %copy-start.1 = (bf16[2,256,1024]{2,1,0:T(8,128)(2,1)S(1)}, bf16[2,256,1024]{2,1,0:T(8,128)(2,1)}, u32[]{:S(2)}) copy-start(bf16[2,256,1024]{2,1,0:T(8,128)(2,1)} %param.15) | copy-start | bytes 3145732
  63.3 3.2 %collective-permute-start.6 = (bf16[2,256,16]{1,0,2:T(2,128)(2,1)S(1)}, bf16[2,256,16]{1,0,2:T(2,128)(2,1)S(1)}, u32[]{:S(2)}, u32[]{:S(2)}) collective-permute-start(bf16[2,256,16]{1,0,2:T(2,128)(2,1)S(1)} %fusion.72), channel_id=1, source_target_pairs={{0,4},{4,8},{8,12},{12,0},{1,5},{5,9},{9,13},{13,1},{2,6},{6,10},{... | collective-permute-start | bytes 49160 | tf_op jit(solution)/shard_map/ppermute | solution.py:20
  64.4 2.8 %collective-permute-start.8 = (bf16[2,256,16]{1,0,2:T(2,128)(2,1)S(1)}, bf16[2,256,16]{1,0,2:T(2,128)(2,1)S(1)}, u32[]{:S(2)}, u32[]{:S(2)}) collective-permute-start(bf16[2,256,16]{1,0,2:T(2,128)(2,1)S(1)} %fusion.72), channel_id=1, source_target_pairs={{4,0},{8,4},{12,8},{0,12},{5,1},{9,5},{13,9},{1,13},{6,2},{10,6},{... | collective-permute-start | bytes 49160 | tf_op jit(solution)/shard_map/ppermute | solution.py:22
  66.5 3.2 %collective-permute-start.7 = (bf16[2,256,16]{1,0,2:T(2,128)(2,1)S(1)}, bf16[2,256,16]{1,0,2:T(2,128)(2,1)S(1)}, u32[]{:S(2)}, u32[]{:S(2)}) collective-permute-start(bf16[2,256,16]{1,0,2:T(2,128)(2,1)S(1)} %collective-permute-done.6), channel_id=1, source_target_pairs={{0,4},{4,8},{8,12},{12,0},{1,5},{5,9},{9,13},{13,1},{2,6},{6,10},{... | collective-permute-start | bytes 49160 | tf_op jit(solution)/shard_map/ppermute | solution.py:20
  78.9 3.2 %collective-permute-start.9 = (bf16[1,256,16]{1,0,2:T(2,128)(2,1)S(1)}, bf16[1,256,16]{1,0,2:T(2,128)(2,1)S(1)}, u32[]{:S(2)}, u32[]{:S(2)}) collective-permute-start(bf16[1,256,16]{1,0,2:T(2,128)(2,1)S(1)} %fusion.90), channel_id=1, source_target_pairs={{0,4},{4,8},{8,12},{12,0},{1,5},{5,9},{9,13},{13,1},{2,6},{6,10},{... | collective-permute-start | bytes 24584 | tf_op jit(solution)/shard_map/ppermute | solution.py:20
  79.3 2.9 %collective-permute-start.11 = (bf16[1,256,16]{1,0,2:T(2,128)(2,1)S(1)}, bf16[1,256,16]{1,0,2:T(2,128)(2,1)S(1)}, u32[]{:S(2)}, u32[]{:S(2)}) collective-permute-start(bf16[1,256,16]{1,0,2:T(2,128)(2,1)S(1)} %fusion.90), channel_id=1, source_target_pairs={{4,0},{8,4},{12,8},{0,12},{5,1},{9,5},{13,9},{1,13},{6,2},{10,6},{... | collective-permute-start | bytes 24584 | tf_op jit(solution)/shard_map/ppermute | solution.py:22
  82.1 3.2 %collective-permute-start.10 = (bf16[1,256,16]{1,0,2:T(2,128)(2,1)S(1)}, bf16[1,256,16]{1,0,2:T(2,128)(2,1)S(1)}, u32[]{:S(2)}, u32[]{:S(2)}) collective-permute-start(bf16[1,256,16]{1,0,2:T(2,128)(2,1)S(1)} %collective-permute-done.9), channel_id=1, source_target_pairs={{0,4},{4,8},{8,12},{12,0},{1,5},{5,9},{9,13},{13,1},{2,6},{6,10},{... | collective-permute-start | bytes 24584 | tf_op jit(solution)/shard_map/ppermute | solution.py:20
  88.4 42.1 %reduce-scatter.15.cloned.1.call-start = ((), (), s32[]{:S(2)}) async-start(), calls=%async_computation.10 | async-start | bytes 81920 | tf_op jit(solution)/shard_map/reduce_scatter | solution.py:98
  110.3 53.2 %reduce-scatter.25.cloned.1.call-start = ((), (), s32[]{:S(2)}) async-start(), calls=%async_computation.15 | async-start | bytes 327680
  136.8 29.9 %copy-start.19 = (s32[4]{0:T(128)S(1)}, s32[4]{0:T(128)}, u32[]{:S(2)}) copy-start(s32[4]{0:T(128)} %get-tuple-element.15) | copy-start | bytes 52
  136.8 30.1 %copy-start.17 = (s32[4]{0:T(128)S(1)}, s32[4]{0:T(128)}, u32[]{:S(2)}) copy-start(s32[4]{0:T(128)} %copy-done.16) | copy-start | bytes 52
  143.3 47.1 %copy-start.9 = (bf16[4,256]{1,0:T(4,128)(2,1)S(1)}, bf16[4,256]{1,0:T(4,128)(2,1)}, u32[]{:S(2)}) copy-start(bf16[4,256]{1,0:T(4,128)(2,1)} %get-tuple-element.19) | copy-start | bytes 6148
  143.4 47.1 %reduce-scatter.17.cloned.1.call-start = ((), (), s32[]{:S(2)}) async-start(), calls=%async_computation.11 | async-start | bytes 163840 | tf_op jit(solution)/shard_map/reduce_scatter | solution.py:98
  166.9 46.0 %copy-start.6 = (f32[4,256]{1,0:T(4,128)S(1)}, f32[4,256]{1,0:T(4,128)}, u32[]{:S(2)}) copy-start(f32[4,256]{1,0:T(4,128)} %copy-done.5) | copy-start | bytes 12292
  167.2 51.3 %copy-start.15 = (s32[4]{0:T(128)S(1)}, s32[4]{0:T(128)}, u32[]{:S(2)}) copy-start(s32[4]{0:T(128)} %copy-done.14) | copy-start | bytes 52
  167.2 51.6 %copy-start.13 = (s32[4]{0:T(128)S(1)}, s32[4]{0:T(128)}, u32[]{:S(2)}) copy-start(s32[4]{0:T(128)} %copy-done.12) | copy-start | bytes 52
  167.2 51.8 %copy-start.11 = (s32[4]{0:T(128)S(1)}, s32[4]{0:T(128)}, u32[]{:S(2)}) copy-start(s32[4]{0:T(128)} %copy-done.10) | copy-start | bytes 52
  170.7 42.1 %reduce-scatter.19.cloned.1.call-start = ((), (), s32[]{:S(2)}) async-start(), calls=%async_computation.12 | async-start | bytes 163840 | tf_op jit(solution)/shard_map/reduce_scatter | solution.py:111
  193.1 51.2 %reduce-scatter.21.cloned.1.call-start = ((), (), s32[]{:S(2)}) async-start(), calls=%async_computation.13 | async-start | bytes 327680 | tf_op jit(solution)/shard_map/reduce_scatter | solution.py:98
  219.2 25.1 %copy-start.8 = (bf16[4,256]{1,0:T(4,128)(2,1)S(1)}, bf16[4,256]{1,0:T(4,128)(2,1)}, u32[]{:S(2)}) copy-start(bf16[4,256]{1,0:T(4,128)(2,1)} %get-tuple-element.2) | copy-start | bytes 6148
  219.4 47.5 %copy-start.4 = (f32[4,256]{1,0:T(4,128)S(1)}, f32[4,256]{1,0:T(4,128)}, u32[]{:S(2)}) copy-start(f32[4,256]{1,0:T(4,128)} %copy-done.3) | copy-start | bytes 12292
  224.1 42.7 %reduce-scatter.23.cloned.1.call-start = ((), (), s32[]{:S(2)}) async-start(), calls=%async_computation.14 | async-start | bytes 327680 | tf_op jit(solution)/shard_map/reduce_scatter | solution.py:111
Sparse Core Ops, SparseCore 0:
  31.8 10.9 reduce-scatter.10
  88.5 19.3 reduce-scatter.12
  111.0 19.4 reduce-scatter.14
  143.5 20.0 reduce-scatter.24
  170.8 19.5 reduce-scatter.16
  193.3 19.5 reduce-scatter.18
  224.2 20.0 reduce-scatter.20
  246.8 20.0 reduce-scatter.22
